TPU v7x, 512 devices: a whole 4x8x8 slice. The times are simulated.
512 devices in a mesh: rows: 32 (over x, y), depth: 16 (over z, core).
Axes of the slice: x: 4, y: 8, z: 8, core: 2. Of those that a mesh axis runs over, the one named last changes fastest.
Arguments:
- left_factors: bfloat16 [32, 32, 2048, 128], P('rows', 'depth'), may hold values from -0.125 to 0.125
- right_factors: bfloat16 [32, 32, 2048, 128], P('rows', 'depth'), may hold values from -0.125 to 0.125
- probe_matrix: bfloat16 [2048, 128], replicated, may hold values from -6 to 6
- tile_list: int32 [32, 4], replicated, may hold values from 0 to 31, all different within a row
Outputs:
- basis: float32 [32, 4, 2048, 128], P('rows', None, 'depth')
- chol_factor: float32 [32, 4, 128, 128], P('rows')
Inputs may be any that keep to these rules, and one draw needn't show every extreme that they name: `tile_list`: each row holds 4 different tile rows, and every tile row is named by some row.
All inputs are finite; a program needn't handle non-finite values.
Results may differ from a plain program's by a relative error of at most 0.0058.
Values may be sent and summed in bfloat16 or wider, within the bound.
A program may use at most 64 MiB of HBM per device.

v0:
```python
import math
import jax
import jax.numpy as jnp
from jax import lax
from jax.sharding import PartitionSpec as P


def on_device(left_factors, right_factors, probe_matrix, tile_list):
    left_own = left_factors[0]
    right_own = right_factors[0]
    panels, tile_size, rank_size = left_own.shape
    scale = math.sqrt(float(tile_size))
    image = jnp.einsum(
        "pbk,bl->pkl", left_own, probe_matrix, preferred_element_type=jnp.float32
    ).astype(jnp.bfloat16)
    sketch_rows = jnp.einsum(
        "pbk,pkl->pbl", right_own, image, preferred_element_type=jnp.float32
    ).astype(jnp.bfloat16)
    sliced = lax.all_to_all(sketch_rows[:, None], "rows", split_axis=2, concat_axis=1, tiled=True)
    readers_order = jnp.transpose(tile_list)
    outgoing = jnp.take(sliced, readers_order, axis=1)
    arrived = lax.all_to_all(outgoing, "rows", split_axis=2, concat_axis=2, tiled=True)
    listed = arrived.shape[1]
    arrived = arrived.reshape(panels, listed, tile_size, rank_size)
    coupling = jnp.einsum(
        "pbk,ptbl->tpkl", right_own, arrived, preferred_element_type=jnp.float32
    ).astype(jnp.bfloat16)
    partial_sketch = jnp.einsum(
        "pbk,tpkl->tbl", left_own, coupling, preferred_element_type=jnp.float32
    )
    block_rows = tile_size // lax.axis_size("depth")
    total = lax.psum(partial_sketch, "depth")
    gram = jnp.einsum("tbk,tbl->tkl", total, total, precision=lax.Precision.HIGHEST)
    start = lax.axis_index("depth") * block_rows
    own_rows = lax.dynamic_slice_in_dim(total, start, block_rows, 1)
    lower = jnp.linalg.cholesky(gram)
    solved = jax.scipy.linalg.solve_triangular(
        lower, jnp.transpose(own_rows, (0, 2, 1)), lower=True
    )
    basis = jnp.transpose(solved, (0, 2, 1)) * scale
    return (basis[None], (lower / scale)[None])


def solution(mesh):
    in_specs = (P("rows", "depth", None, None), P("rows", "depth", None, None), P(), P())
    out_specs = (P("rows", None, "depth", None), P("rows", None, None, None))
    return jax.shard_map(
        on_device, mesh=mesh, in_specs=in_specs, out_specs=out_specs, check_vma=False
    )
```

profile of v0, /device:TPU:1, one launch (start us, length us, event | category | flops | bytes accessed | tf_op | source)
XLA Modules:
  0.0 398.3 jit_solution(8953928017421091047)
XLA Ops:
  7.2 0.0 copy-start
  7.2 1.2 copy-done
  8.4 0.0 copy-start.2
  8.4 2.3 fusion.3
  10.7 2.0 copy.31
  12.7 10.5 %all-to-all-start = ((bf16[2,1,2048,128]{3,0,1,2:T(2,128)(2,1)}), bf16[2,1,2048,128]{3,0,1,2:T(2,128)(2,1)S(1)}, u32[]{:S(2)}, u32[]{:S(2)}) async-start(bf16[2,1,2048,128]{3,0,1,2:T(2,128)(2,1)} %copy.31), calls=%async_computation | async-start | bytes 2097152 | tf_op jit(solution)/shard_map/all_to_all | solution.py:19
  23.2 0.0 all-reduce.2.cloned.1.call-start
  23.2 0.0 copy-done.2
  23.3 0.1 reshape.29
  23.4 0.1 copy.28
  23.5 24.3 %all-to-all-done = bf16[2,1,2048,128]{3,0,1,2:T(2,128)(2,1)S(1)} async-done(((bf16[2,1,2048,128]{3,0,1,2:T(2,128)(2,1)}), bf16[2,1,2048,128]{3,0,1,2:T(2,128)(2,1)S(1)}, u32[]{:S(2)}, u32[]{:S(2)}) %all-to-all-start) | async-done | bytes 1048608 | tf_op jit(solution)/shard_map/all_to_all | solution.py:19
  47.8 0.1 copy.32
  48.0 3.0 gather_fusion
  51.0 2.5 fusion.2
  53.5 100.6 %all_to_all.17 = bf16[2,4,32,64,128]{4,3,1,0,2:T(8,128)(2,1)S(1)} all-to-all(bf16[2,4,32,64,128]{4,3,1,0,2:T(8,128)(2,1)S(1)} %fusion.2), channel_id=1, replica_groups=mesh['rows'=32,'depth'=16] {'rows'}, dimensions={2} | all-to-all | bytes 8388608 | tf_op jit(solution)/shard_map/all_to_all | solution.py:22
  154.1 0.0 copy-start.1
  154.1 2.9 copy.34
  157.0 0.0 copy-done.1
  157.0 6.1 %convolution_bitcast_fusion = f32[4,2048,128]{1,2,0:T(8,128)} fusion(bf16[1,2,2048,128]{3,2,1,0:T(8,128)(2,1)S(1)} %copy-done, bf16[2,4,2048,128]{3,2,1,0:T(8,128)(2,1)} %bitcast.58, bf16[1,2,2048,128]{3,2,1,0:T(8,128)(2,1)S(1)} %copy-done.1), kind=kOutput, calls=%fused_computation.5 | convolution fusion | flops 1073872896 | bytes 10485760 | tf_op jit(solution)/shard_map/pbk,tpkl->tbl/dot_general | solution.py:28
  163.2 0.0 all-reduce.2.cloned.1.call-update
  163.2 131.2 %all-reduce.2.cloned.1.call-done = f32[4,2048,128]{1,2,0:T(8,128)} async-done(((f32[4,2048,128]{1,2,0:T(8,128)}), f32[4,2048,128]{1,2,0:T(8,128)}) %all-reduce.2.cloned.1.call-update) | async-done | bytes 4194320 | tf_op jit(solution)/shard_map/psum | solution.py:32
  294.5 7.4 %fusion.26 = f32[4,128,128]{2,1,0:T(8,128)S(1)} fusion(f32[4,2048,128]{1,2,0:T(8,128)} %all-reduce.2.cloned.1.call-done), kind=kOutput, calls=%fused_computation.33 | convolution fusion | flops 1610612736 | bytes 4456448 | tf_op jit(solution)/shard_map/tbk,tbl->tkl/dot_general | solution.py:33
  301.9 0.1 copy.37
  302.0 46.9 %custom-call.8 = f32[4,128,128]{2,1,0:T(8,128)S(1)} custom-call(f32[4,128,128]{2,1,0:T(8,128)S(1)} %fusion.23), custom_call_target="Cholesky" | custom-call | tf_op jit(solution)/shard_map/jit(cholesky)/cholesky | solution.py:36
  349.0 0.1 compare_reduce_fusion
  349.1 0.8 multiply_bitcast_fusion
  349.9 39.3 %custom-call.9 = f32[4,1,128,128]{2,3,1,0:T(8,128)S(1)} custom-call(f32[4,1,128,128]{3,2,1,0:T(8,128)S(1)} %get-tuple-element.3), custom_call_target="InvertDiagBlocksLowerTriangular" | custom-call | tf_op jit(solution)/shard_map/jit(_solve_triangular)/vmap()/triangular_solve | solution.py:37
  389.2 2.3 fusion.10
  (7 shorter events, 0.1 us)
Async XLA Ops:
  7.2 1.2 copy-start
  8.4 14.8 %copy-start.2 = (s32[32,4]{0,1:T(4,128)S(1)}, s32[32,4]{0,1:T(4,128)}, u32[]{:S(2)}) copy-start(s32[32,4]{0,1:T(4,128)} %param.7) | copy-start | bytes 1540
  12.7 35.1 %all-to-all-start = ((bf16[2,1,2048,128]{3,0,1,2:T(2,128)(2,1)}), bf16[2,1,2048,128]{3,0,1,2:T(2,128)(2,1)S(1)}, u32[]{:S(2)}, u32[]{:S(2)}) async-start(bf16[2,1,2048,128]{3,0,1,2:T(2,128)(2,1)} %copy.31), calls=%async_computation | async-start | bytes 2097152 | tf_op jit(solution)/shard_map/all_to_all | solution.py:19
  23.2 271.3 %all-reduce.2.cloned.1.call-start = ((), (), s32[]{:S(2)}) async-start(), calls=%async_computation.2 | async-start | bytes 8388608 | tf_op jit(solution)/shard_map/psum | solution.py:32
  154.1 3.0 copy-start.1
Sparse Core Ops, SparseCore 0:
  163.3 131.1 all-reduce.1
where the time goes:
time: 399 us; the launch traced here: 398 us
  waiting for transfers between devices  156 us (39%)
  blocking collectives  101 us (25%)
  other arithmetic  89.8 us (23%)
  matrix products  18.1 us (5%)
  between operations  14.1 us (4%)
  starting transfers between devices  10.5 us (3%)
  local copies, waits for them, and re-layouts  9.65 us (2%)
    psum x1, waiting for transfers between devices, on_device(): total = lax.psum(partial_sketch, 'depth')  131 us
    all_to_all x1, blocking collectives, on_device(): lax.all_to_all(outgoing, 'rows', split_axis=2, concat_axis=2, tiled=True)  101 us
    another operation x4, other arithmetic, on_device(): lower = jnp.linalg.cholesky(gram)  47.1 us
    another operation x2, other arithmetic, on_device(): jax.scipy.linalg.solve_triangular(lower, jnp.transpose(own_rows, (0, 2, 1...  39.3 us
    all_to_all x1, waiting for transfers between devices, on_device(): lax.all_to_all(sketch_rows[:, None], 'rows', split_axis=2, concat_axis=1,...  24.3 us
    all_to_all x1, starting transfers between devices, on_device(): lax.all_to_all(sketch_rows[:, None], 'rows', split_axis=2, concat_axis=1,...  10.5 us
  transfers between devices with their start and end apart: 2, of which 2 were waited for; matrix products, arithmetic and copies ran while one was open for 0% of the time, Pallas kernels for 0%

commit v1 on v0

--- a/solution.py
+++ b/solution.py
@@ -29,7 +29,9 @@
         "pbk,tpkl->tbl", left_own, coupling, preferred_element_type=jnp.float32
     )
     block_rows = tile_size // lax.axis_size("depth")
-    total = lax.psum(partial_sketch, "depth")
+    total = partial_sketch
+    for hop in (1, 2, 4, 8):
+        total = total + lax.ppermute(total, "depth", [(dev, dev ^ hop) for dev in range(16)])
     gram = jnp.einsum("tbk,tbl->tkl", total, total, precision=lax.Precision.HIGHEST)
     start = lax.axis_index("depth") * block_rows
     own_rows = lax.dynamic_slice_in_dim(total, start, block_rows, 1)

time: 399 us -> 747 us (1.87)
  waiting for transfers between devices: 156 us -> 482 us
  starting transfers between devices: 10.5 us -> 35.4 us
  between operations: 14.1 us -> 0.79 us
  other arithmetic: 89.8 us -> 101 us
    ppermute x0 -> x4, waiting for transfers between devices: none -> 458 us  [on_device(): lax.ppermute(total, 'depth', [(dev, dev ^ hop) for dev in range(16)])]
    psum x1 -> x0, waiting for transfers between devices: 131 us -> none  [on_device(): total = lax.psum(partial_sketch, 'depth')]
    ppermute x0 -> x4, starting transfers between devices: none -> 24.9 us  [on_device(): lax.ppermute(total, 'depth', [(dev, dev ^ hop) for dev in range(16)])]
    add x0 -> x4, other arithmetic: none -> 10.9 us  [on_device(): total + lax.ppermute(total, 'depth', [(dev, dev ^ hop) for dev in range(1...]
  transfers between devices with their start and end apart: 2 -> 5, of which waited for: 2 -> 5; matrix products, arithmetic and copies ran while one was open for 0% -> 0% of each run, Pallas kernels for 0% -> 0%
where the time goes in v1:
time: 747 us; the launch traced here: 746 us
  waiting for transfers between devices  482 us (65%)
  other arithmetic  101 us (14%)
  blocking collectives  101 us (14%)
  starting transfers between devices  35.4 us (5%)
  matrix products  14.7 us (2%)
  local copies, waits for them, and re-layouts  11.5 us (2%)
    ppermute x4, waiting for transfers between devices, on_device(): lax.ppermute(total, 'depth', [(dev, dev ^ hop) for dev in range(16)])  458 us
    all_to_all x1, blocking collectives, on_device(): lax.all_to_all(outgoing, 'rows', split_axis=2, concat_axis=2, tiled=True)  101 us
    another operation x4, other arithmetic, on_device(): lower = jnp.linalg.cholesky(gram)  47.1 us
    another operation x2, other arithmetic, on_device(): jax.scipy.linalg.solve_triangular(lower, jnp.transpose(own_rows, (0, 2, 1...  39.3 us
    ppermute x4, starting transfers between devices, on_device(): lax.ppermute(total, 'depth', [(dev, dev ^ hop) for dev in range(16)])  24.9 us
    all_to_all x1, waiting for transfers between devices, on_device(): lax.all_to_all(sketch_rows[:, None], 'rows', split_axis=2, concat_axis=1,...  24.4 us
  transfers between devices with their start and end apart: 5, of which 5 were waited for; matrix products, arithmetic and copies ran while one was open for 0% of the time, Pallas kernels for 0%

profile of v1, /device:TPU:1, one launch (start us, length us, event | category | flops | bytes accessed | tf_op | source)
XLA Modules:
  0.0 745.9 jit_solution(7146306681799015975)
XLA Ops:
  0.6 0.0 copy-start
  0.6 1.2 copy-done
  1.9 0.0 copy-start.3
  1.9 2.3 fusion.3
  4.2 2.0 copy.31
  6.2 10.5 %all-to-all-start = ((bf16[2,1,2048,128]{3,0,1,2:T(2,128)(2,1)}), bf16[2,1,2048,128]{3,0,1,2:T(2,128)(2,1)S(1)}, u32[]{:S(2)}, u32[]{:S(2)}) async-start(bf16[2,1,2048,128]{3,0,1,2:T(2,128)(2,1)} %copy.31), calls=%async_computation | async-start | bytes 2097152 | tf_op jit(solution)/shard_map/all_to_all | solution.py:19
  16.7 0.0 copy-done.3
  16.7 0.1 reshape.29
  16.8 0.1 copy.28
  16.9 24.4 %all-to-all-done = bf16[2,1,2048,128]{3,0,1,2:T(2,128)(2,1)S(1)} async-done(((bf16[2,1,2048,128]{3,0,1,2:T(2,128)(2,1)}), bf16[2,1,2048,128]{3,0,1,2:T(2,128)(2,1)S(1)}, u32[]{:S(2)}, u32[]{:S(2)}) %all-to-all-start) | async-done | bytes 1048608 | tf_op jit(solution)/shard_map/all_to_all | solution.py:19
  41.3 0.1 copy.32
  41.4 3.0 gather_fusion
  44.4 2.5 fusion.2
  47.0 100.6 %all_to_all.17 = bf16[2,4,32,64,128]{4,3,1,0,2:T(8,128)(2,1)S(1)} all-to-all(bf16[2,4,32,64,128]{4,3,1,0,2:T(8,128)(2,1)S(1)} %fusion.2), channel_id=1, replica_groups=mesh['rows'=32,'depth'=16] {'rows'}, dimensions={2} | all-to-all | bytes 8388608 | tf_op jit(solution)/shard_map/all_to_all | solution.py:22
  147.5 0.0 copy-start.2
  147.5 2.9 copy.34
  150.4 0.0 copy-done.2
  150.4 6.2 convolution_bitcast_fusion
  156.6 6.9 collective-permute-start
  163.5 7.0 collective-permute-done
  170.5 2.9 add.37
  173.4 4.0 collective-permute-start.1
  177.4 90.6 %collective-permute-done.1 = f32[4,2048,128]{1,2,0:T(8,128)S(1)} collective-permute-done((f32[4,2048,128]{1,2,0:T(8,128)S(1)}, f32[4,2048,128]{1,2,0:T(8,128)S(1)}, u32[]{:S(2)}, u32[]{:S(2)}) %collective-permute-start.1) | collective-permute-done | bytes 4194336 | tf_op jit(solution)/shard_map/ppermute | solution.py:34
  268.1 1.1 add.38
  269.2 5.8 collective-permute-start.2
  275.0 180.0 %collective-permute-done.2 = f32[4,2048,128]{1,2,0:T(8,128)S(1)} collective-permute-done((f32[4,2048,128]{1,2,0:T(8,128)S(1)}, f32[4,2048,128]{1,2,0:T(8,128)S(1)}, u32[]{:S(2)}, u32[]{:S(2)}) %collective-permute-start.2) | collective-permute-done | bytes 4194336 | tf_op jit(solution)/shard_map/ppermute | solution.py:34
  455.0 2.7 add.39
  457.7 8.2 %collective-permute-start.3 = (f32[4,2048,128]{1,2,0:T(8,128)}, f32[4,2048,128]{1,2,0:T(8,128)}, u32[]{:S(2)}, u32[]{:S(2)}) collective-permute-start(f32[4,2048,128]{1,2,0:T(8,128)} %add.39), channel_id=1, source_target_pairs={{0,8},{1,9},{2,10},{3,11},{4,12},{5,13},{6,14},{7,15},{8,0},{9,1},... | collective-permute-start | bytes 12582920 | tf_op jit(solution)/shard_map/ppermute | solution.py:34
  465.9 180.2 %collective-permute-done.3 = f32[4,2048,128]{1,2,0:T(8,128)} collective-permute-done((f32[4,2048,128]{1,2,0:T(8,128)}, f32[4,2048,128]{1,2,0:T(8,128)}, u32[]{:S(2)}, u32[]{:S(2)}) %collective-permute-start.3) | collective-permute-done | bytes 4194336 | tf_op jit(solution)/shard_map/ppermute | solution.py:34
  646.2 4.2 add.40
  650.4 0.0 copy-start.1
  650.4 1.9 copy-done.1
  652.3 3.9 fusion.26
  656.3 0.1 copy.37
  656.4 46.9 %custom-call.8 = f32[4,128,128]{2,1,0:T(8,128)S(1)} custom-call(f32[4,128,128]{2,1,0:T(8,128)S(1)} %fusion.23), custom_call_target="Cholesky" | custom-call | tf_op jit(solution)/shard_map/jit(cholesky)/cholesky | solution.py:38
  703.4 0.1 compare_reduce_fusion
  703.5 0.8 multiply_bitcast_fusion
  704.3 39.3 %custom-call.9 = f32[4,1,128,128]{2,3,1,0:T(8,128)S(1)} custom-call(f32[4,1,128,128]{3,2,1,0:T(8,128)S(1)} %get-tuple-element.3), custom_call_target="InvertDiagBlocksLowerTriangular" | custom-call | tf_op jit(solution)/shard_map/jit(_solve_triangular)/vmap()/triangular_solve | solution.py:39
  743.6 2.3 fusion.10
  (7 shorter events, 0.1 us)
Async XLA Ops:
  0.6 1.2 copy-start
  1.9 14.8 %copy-start.3 = (s32[32,4]{0,1:T(4,128)S(1)}, s32[32,4]{0,1:T(4,128)}, u32[]{:S(2)}) copy-start(s32[32,4]{0,1:T(4,128)} %param.7) | copy-start | bytes 1540
  6.2 35.1 %all-to-all-start = ((bf16[2,1,2048,128]{3,0,1,2:T(2,128)(2,1)}), bf16[2,1,2048,128]{3,0,1,2:T(2,128)(2,1)S(1)}, u32[]{:S(2)}, u32[]{:S(2)}) async-start(bf16[2,1,2048,128]{3,0,1,2:T(2,128)(2,1)} %copy.31), calls=%async_computation | async-start | bytes 2097152 | tf_op jit(solution)/shard_map/all_to_all | solution.py:19
  147.5 2.9 copy-start.2
  156.6 13.9 %collective-permute-start = (f32[4,2048,128]{1,2,0:T(8,128)}, f32[4,2048,128]{1,2,0:T(8,128)S(1)}, u32[]{:S(2)}, u32[]{:S(2)}) collective-permute-start(f32[4,2048,128]{1,2,0:T(8,128)} %convolution_bitcast_fusion), channel_id=1, source_target_pairs={{0,1},{1,0},{2,3},{3,2},{4,5},{5,4},{6,7},{7,6},{8,9},{9,8},{10,11... | collective-permute-start | bytes 12582920 | tf_op jit(solution)/shard_map/ppermute | solution.py:34
  173.4 94.6 %collective-permute-start.1 = (f32[4,2048,128]{1,2,0:T(8,128)S(1)}, f32[4,2048,128]{1,2,0:T(8,128)S(1)}, u32[]{:S(2)}, u32[]{:S(2)}) collective-permute-start(f32[4,2048,128]{1,2,0:T(8,128)S(1)} %add.37), channel_id=1, source_target_pairs={{0,2},{1,3},{2,0},{3,1},{4,6},{5,7},{6,4},{7,5},{8,10},{9,11},{10,... | collective-permute-start | bytes 12582920 | tf_op jit(solution)/shard_map/ppermute | solution.py:34
  269.2 185.9 %collective-permute-start.2 = (f32[4,2048,128]{1,2,0:T(8,128)S(1)}, f32[4,2048,128]{1,2,0:T(8,128)S(1)}, u32[]{:S(2)}, u32[]{:S(2)}) collective-permute-start(f32[4,2048,128]{1,2,0:T(8,128)S(1)} %add.38), channel_id=1, source_target_pairs={{0,4},{1,5},{2,6},{3,7},{4,0},{5,1},{6,2},{7,3},{8,12},{9,13},{10,... | collective-permute-start | bytes 12582920 | tf_op jit(solution)/shard_map/ppermute | solution.py:34
  457.7 188.5 %collective-permute-start.3 = (f32[4,2048,128]{1,2,0:T(8,128)}, f32[4,2048,128]{1,2,0:T(8,128)}, u32[]{:S(2)}, u32[]{:S(2)}) collective-permute-start(f32[4,2048,128]{1,2,0:T(8,128)} %add.39), channel_id=1, source_target_pairs={{0,8},{1,9},{2,10},{3,11},{4,12},{5,13},{6,14},{7,15},{8,0},{9,1},... | collective-permute-start | bytes 12582920 | tf_op jit(solution)/shard_map/ppermute | solution.py:34
  650.4 1.9 copy-start.1
